TPU v7x, 512 devices: a whole 4x8x8 slice. The times are simulated.
512 devices in a mesh: dp: 32 (over z, x), tensor: 16 (over y, core).
Axes of the slice: x: 4, y: 8, z: 8, core: 2. Of those that a mesh axis runs over, the one named last changes fastest.
Arguments:
- features: bfloat16 [32768, 8192], P('dp', 'tensor'), may hold values from -6 to 6
- key_value_weight: bfloat16 [8192, 2048], P(None, 'tensor'), may hold values from -0.0625 to 0.0625
- adapter_down_factors: bfloat16 [8192, 16, 128], P(None, None, 'tensor'), may hold values from -0.0625 to 0.0625
- adapter_up_factors: bfloat16 [16, 128, 2048], P(None, None, 'tensor'), may hold values from -0.5 to 0.5
- row_adapter_index: int32 [32768], P('dp'), may hold values from 0 to 15, never falling along the last dimension, each value on 1 to 4096 neighbouring positions
- ranks: int32 [16], replicated, may hold values from 8 to 128, as said below
Outputs:
- projected: bfloat16 [32768, 2048], P('dp', 'tensor')
Inputs may be any that keep to these rules, and one draw needn't show every extreme that they name: `ranks`: every rank is 128 // 16 times a power of two from 1 to 16; some adapter has rank 128. `row_adapter_index`: ids never fall along the rows.
All inputs are finite; a program needn't handle non-finite values.
Results may differ from a plain program's by a relative error of at most 0.0033.
Values may be sent and summed in bfloat16 or wider, within the bound.
A program may use at most 64 MiB of HBM per device.

v0:
```python
import jax
import jax.numpy as jnp
from jax import lax
from jax.sharding import PartitionSpec as P


def body(
    features, key_value_weight, adapter_down_factors, adapter_up_factors, row_adapter_index, ranks
):
    rows = features.shape[0]
    input_width = key_value_weight.shape[0]
    output_columns = key_value_weight.shape[1]
    adapter_count = adapter_down_factors.shape[1]
    rank_window = adapter_down_factors.shape[2]
    padded_rank_total = adapter_up_factors.shape[1]
    flattened_down_factors = adapter_down_factors.reshape(input_width, adapter_count * rank_window)
    piece = lax.all_gather(features, "tensor", axis=1, tiled=True)
    base = jnp.dot(piece, key_value_weight, preferred_element_type=jnp.float32)
    intermediate_state = jnp.dot(piece, flattened_down_factors, preferred_element_type=jnp.float32)
    onehot = (
        row_adapter_index[:, None] == jnp.arange(adapter_count, dtype=jnp.int32)[None, :]
    ).astype(jnp.float32)
    row_rank = jnp.sum(onehot * ranks[None, :].astype(jnp.float32), axis=1)
    chosen = jnp.sum(
        intermediate_state.reshape(rows, adapter_count, rank_window) * onehot[:, :, None], axis=1
    )
    offset = lax.axis_index("tensor") * rank_window
    position = (offset + jnp.arange(rank_window, dtype=jnp.int32)).astype(jnp.float32)[None, :]
    local_low = jnp.where(position < row_rank[:, None], chosen, 0.0).astype(jnp.bfloat16)
    low = lax.all_gather(local_low, "tensor", axis=1, tiled=True)
    broadcast_rows = (
        (low.astype(jnp.float32)[:, None, :] * onehot[:, :, None])
        .reshape(rows, adapter_count * padded_rank_total)
        .astype(jnp.bfloat16)
    )
    lowrank_update = jnp.dot(
        broadcast_rows,
        adapter_up_factors.reshape(adapter_count * padded_rank_total, output_columns),
        preferred_element_type=jnp.float32,
    )
    scaled = 4.0 / jnp.sqrt(row_rank)
    return (base + scaled[:, None] * lowrank_update).astype(jnp.bfloat16)


def solution(mesh):
    in_specs = (
        P("dp", "tensor"),
        P(None, "tensor"),
        P(None, None, "tensor"),
        P(None, None, "tensor"),
        P("dp"),
        P(),
    )
    out_specs = P("dp", "tensor")
    return jax.shard_map(body, mesh=mesh, in_specs=in_specs, out_specs=out_specs, check_vma=False)
```

profile of v0, /device:TPU:1, one launch (start us, length us, event | category | flops | bytes accessed | tf_op | source)
XLA Modules:
  0.0 160.5 jit_solution(8877212561154451695)
XLA Ops:
  6.5 0.0 copy-start
  6.5 0.0 all-gather.2.cloned.1.call-start
  6.5 0.7 all-gather.2.cloned.1.call-update
  7.3 0.7 convert_element_type.31
  7.9 0.8 select_reduce_fusion
  8.7 0.7 fusion.20
  9.4 103.7 %all-gather.2.cloned.1.call-done = bf16[1024,8192]{1,0:T(8,128)(2,1)} async-done(((bf16[1024,512]{1,0:T(8,128)(2,1)}), bf16[1024,8192]{1,0:T(8,128)(2,1)}) %all-gather.2.cloned.1.call-update) | async-done | bytes 16777232 | tf_op jit(solution)/shard_map/all_gather | solution.py:17
  113.1 0.0 copy-done
  113.1 11.5 %fusion.15 = bf16[1024,8]{0,1:T(8,128)(2,1)S(1)} fusion(bf16[16,8,8192]{2,1,0:T(8,128)(2,1)S(1)} %bitcast.23, bf16[1024,8192]{1,0:T(8,128)(2,1)} %all-gather.2.cloned.1.call-done, f32[1024,16]{0,1:T(8,128)S(1)} %fusion.20), kind=kOutput, calls=%fused_computation.12 | convolution fusion | flops 2147737600 | bytes 18956288 | tf_op jit(solution)/shard_map/dot_general | solution.py:19
  124.7 0.1 select_convert_fusion
  124.7 16.3 %all_gather.7 = bf16[1024,128]{0,1:T(8,128)(2,1)S(1)} all-gather(bf16[1024,8]{0,1:T(8,128)(2,1)S(1)} %select_convert_fusion), channel_id=1, replica_groups=mesh['dp'=32,'tensor'=16] {'tensor'}, dimensions={1}, use_global_device_ids=true | all-gather | bytes 278528 | tf_op jit(solution)/shard_map/all_gather | solution.py:30
  141.1 0.1 copy.14
  141.2 0.0 copy-start.1
  141.2 8.8 %fusion.21 = f32[1024,128]{1,0:T(8,128)S(1)} fusion(bf16[1024,8192]{1,0:T(8,128)(2,1)} %all-gather.2.cloned.1.call-done, bf16[8192,128]{1,0:T(8,128)(2,1)} %param.7), kind=kOutput, calls=%fused_computation.19 | convolution fusion | flops 2147483648 | bytes 19398656 | tf_op jit(solution)/shard_map/dot_general | solution.py:18
  150.0 0.0 copy-done.1
  150.0 3.7 %fusion.14 = bf16[1024,128]{1,0:T(8,128)(2,1)} fusion(f32[1024,128]{1,0:T(8,128)S(1)} %fusion.21, bf16[16,128,128]{2,1,0:T(8,128)(2,1)S(1)} %copy-done.1, f32[1024,16]{0,1:T(8,128)S(1)} %fusion.20, f32[1024,128]{1,0:T(8,128)S(1)} %copy.14, f32[1024]{0:T(1024)S(1)} %rsqrt_multiply_fusion), kind=kOutput, calls=%fused_computation.11 | convolution fusion | flops 541458432 | bytes 1904640 | tf_op jit(solution)/shard_map/dot_general | solution.py:36
  (2 shorter events, 0.0 us)
Async XLA Ops:
  6.5 106.6 %copy-start = (bf16[8192,16,8]{0,2,1:T(8,128)(2,1)S(1)}, bf16[8192,16,8]{0,2,1:T(8,128)(2,1)}, u32[]{:S(2)}) copy-start(bf16[8192,16,8]{0,2,1:T(8,128)(2,1)} %param.8) | copy-start | bytes 6291460
  6.5 106.6 %all-gather.2.cloned.1.call-start = ((), (), s32[]{:S(2)}) async-start(), calls=%async_computation | async-start | bytes 17825792 | tf_op jit(solution)/shard_map/all_gather | solution.py:17
  141.2 8.8 %copy-start.1 = (bf16[16,128,128]{2,1,0:T(8,128)(2,1)S(1)}, bf16[16,128,128]{2,1,0:T(8,128)(2,1)}, u32[]{:S(2)}) copy-start(bf16[16,128,128]{2,1,0:T(8,128)(2,1)} %param.9) | copy-start | bytes 1572868
Sparse Core Ops, SparseCore 0:
  9.5 103.5 all-gather.1
where the time goes:
time: 161 us
  waiting for transfers between devices  104 us (65%)
  matrix products  24 us (15%)
  blocking collectives  16.3 us (10%)
  between operations  13.4 us (8%)
  other arithmetic  2.21 us (1%)
    all_gather x1, waiting for transfers between devices, body(): piece = lax.all_gather(features, 'tensor', axis=1, tiled=True)  104 us
    all_gather x1, blocking collectives, body(): low = lax.all_gather(local_low, 'tensor', axis=1, tiled=True)  16.3 us
    dot_general x1, matrix products, body(): jnp.dot(piece, flattened_down_factors, preferred_element_type=jnp.float32)  11.5 us
    dot_general x1, matrix products, body(): base = jnp.dot(piece, key_value_weight, preferred_element_type=jnp.float32)  8.77 us
    dot_general x1, matrix products, body(): jnp.dot(broadcast_rows, adapter_up_factors.reshape(adapter_count * padded...  3.68 us
  transfers between devices with their start and end apart: 1, of which 1 were waited for; matrix products, arithmetic and copies ran while one was open for 1% of the time, Pallas kernels for 0%

commit v1 on v0

v1 whole, which is shorter than its diff:
```python
import functools

import jax
import jax.numpy as jnp
from jax import lax
from jax.experimental import pallas as pl
from jax.experimental.pallas import tpu as pltpu
from jax.sharding import PartitionSpec as P

MESH = pl.DeviceIdType.MESH
NX, NY, NZ, NT = 4, 8, 8, 16
ROWS = 1024
HALF = ROWS // 2
KB = 1024
KX = KB // NX
COLS = 128
ADAPTERS, RANK = 16, 128
LOWROWS = ROWS // NT
TILE = 256

OFFSETS = (4, 3, -3, 2, -2, 1, -1, 0)
OWN = 7
UP, DOWN = (0, 1, 3, 5), (0, 2, 4, 6)
LONG = (0, 1)
X_HOPS = (1, -1, 2)


def mod(value, size):
    return lax.rem(value + size, size)


def kernel(
    feat_hbm,
    weight_hbm,
    down_hbm,
    up_hbm,
    index_ref,
    ranks_ref,
    out_ref,
    feat,
    weight,
    down,
    up,
    send16,
    send32,
    recv16,
    recv32,
    row_adapter,
    row_rank,
    low_sum,
    low_send,
    low_recv,
    low,
    local_sem,
    feat_sem,
    wy_sem,
    wx_sem,
    dy_sem,
    dx_sem,
    dz_sem,
    sum_sem,
    lr_sem,
    lg_sem,
):
    g, t = lax.axis_index("dp"), lax.axis_index("tensor")
    z, x = lax.div(g, NX), lax.rem(g, NX)
    y, c = lax.div(t, 2), lax.rem(t, 2)

    def at(dz=0, dx=0, dy=0, dt=0):
        if dt:
            return (g, mod(t + dt, NT))
        return (mod(z + dz, NZ) * NX + mod(x + dx, NX), mod(y + dy, NY) * 2 + c)

    sibling = (g, y * 2 + 1 - c)

    barrier = pltpu.get_barrier_semaphore()
    for d in range(1, NT):
        pl.semaphore_signal(barrier, inc=1, device_id=at(dt=d), device_id_type=MESH)
    for d in X_HOPS:
        pl.semaphore_signal(barrier, inc=1, device_id=at(dx=d), device_id_type=MESH)
    for d in (1, -1):
        pl.semaphore_signal(barrier, inc=1, device_id=at(dz=d), device_id_type=MESH)

    def local(n, src, dst):
        return pltpu.make_async_copy(src, dst, local_sem.at[n])

    def remote(src, dst, sems, n, device):
        return pltpu.make_async_remote_copy(
            src_ref=src,
            dst_ref=dst,
            send_sem=sems.at[(0, *n)],
            recv_sem=sems.at[(1, *n)],
            device_id=device,
            device_id_type=MESH,
        )

    my_k = pl.ds(pl.multiple_of(x * KX, KX), KX)
    half_k = pl.ds(pl.multiple_of(c * (KB // 2), KB // 2), KB // 2)
    my_w = pl.ds(pl.multiple_of(y * KB + x * KX, KX), KX)
    my_d = pl.ds(pl.multiple_of(z * 16, 16), 16)
    locals_ = [
        local(0, feat_hbm, feat.at[:, half_k]),
        local(1, weight_hbm.at[my_w, :], weight.at[OWN, my_k, :]),
        local(2, down_hbm.at[my_d, my_w], down.at[z, pl.ds(pl.multiple_of(y * 16, 16), 16), my_k]),
        local(3, up_hbm, up),
    ]
    for copy in locals_:
        copy.start()

    for r in range(ROWS // 128):
        ids = index_ref[r : r + 1, :].astype(jnp.float32)
        spread = jnp.transpose(jnp.broadcast_to(ids, (128, 128)))
        row_adapter[128 * r : 128 * (r + 1), :] = spread.astype(jnp.int32)

    @pl.loop(0, ROWS // 128)
    def _(r):
        rows = pl.ds(pl.multiple_of(r * 128, 128), 128)
        ids = row_adapter[rows, :]
        rank = jnp.zeros((128, 128), jnp.float32)
        for a in range(ADAPTERS):
            rank = jnp.where(ids == a, ranks_ref[a].astype(jnp.float32), rank)
        row_rank[rows, :] = rank
        low_sum[rows, :] = jnp.zeros((128, 128), jnp.float32)

    pl.semaphore_wait(barrier, NT - 1 + len(X_HOPS) + 2)

    feat_copy = remote(feat_hbm, feat.at[:, half_k], feat_sem, (), sibling)

    def wy(i):
        to = mod(y - OFFSETS[i], NY)
        src = weight_hbm.at[pl.ds(pl.multiple_of(to * KB + x * KX, KX), KX), :]
        return remote(src, weight.at[i, my_k, :], wy_sem, (i,), at(dy=-OFFSETS[i]))

    def wx(i, n):
        part = weight.at[i, my_k, :]
        return remote(part, part, wx_sem, (i, n), at(dx=X_HOPS[n]))

    def dy(i):
        to = mod(y - OFFSETS[i], NY)
        src = down_hbm.at[my_d, pl.ds(pl.multiple_of(to * KB + x * KX, KX), KX)]
        dst = down.at[z, pl.ds(pl.multiple_of(y * 16, 16), 16), my_k]
        return remote(src, dst, dy_sem, (i,), at(dy=-OFFSETS[i]))

    def dx(n):
        part = down.at[z, :, my_k]
        return remote(part, part, dx_sem, (n,), at(dx=X_HOPS[n]))

    def dz(way, hop, q):
        sign = 1 - 2 * way
        part = down.at[mod(z - sign * hop, NZ), 64 * q : 64 * (q + 1), :]
        return remote(part, part, dz_sem, (way, hop, q), at(dz=sign))

    def rs(way, step, half):
        rows = pl.ds(half * HALF, HALF)
        src, dst = (send32, recv32) if step == 3 else (send16, recv16)
        pos = (way, rows) if step == 3 else (way, step, rows)
        return remote(
            src.at[pos], dst.at[pos], sum_sem, (way, step, half), at(dy=1 - 2 * way)
        )

    def lr(d):
        to = mod(t + d, NT)
        src = low_send.at[pl.ds(pl.multiple_of(to * LOWROWS, LOWROWS), LOWROWS), :]
        return remote(src, low_recv.at[d], lr_sem, (d,), at(dt=d))

    my_low = pl.ds(pl.multiple_of(t * LOWROWS, LOWROWS), LOWROWS)

    def lg(d):
        part = low.at[my_low, :]
        return remote(part, part, lg_sem, (d,), at(dt=d))

    sent = []

    def start(copy):
        copy.start()
        sent.append(copy)

    def tiles(half):
        return range(half * HALF, (half + 1) * HALF, TILE)

    def pass_w(i):
        if i == OWN:
            locals_[1].wait()
        else:
            wy(i).wait_recv()
        for n in range(3):
            start(wx(i, n))

    def have_w(i):
        for n in range(3):
            wx(i, n).wait_recv()

    def add_up(i, way, step, half):
        before = step >= 2 or (step == 1 and half == LONG[way])
        if before:
            rs(way, step - 1, half).wait_recv()

        @pl.loop(0, HALF // TILE)
        def _(n):
            rows = pl.ds(pl.multiple_of(half * HALF + n * TILE, TILE), TILE)
            part = jnp.dot(feat[rows, :], weight[i], preferred_element_type=jnp.float32)
            if before:
                part = part + recv16[way, step - 1, rows, :].astype(jnp.float32)
            if step == 3:
                send32[way, rows, :] = part
            else:
                send16[way, step, rows, :] = part.astype(jnp.bfloat16)

        start(rs(way, step, half))

    lane = lax.broadcasted_iota(jnp.int32, (TILE, 128), 1)
    lane_pair = lax.rem(lax.div(lane, 8), 2)

    def low_part(source):
        @pl.loop(0, ROWS // TILE)
        def _(n):
            rows = pl.ds(pl.multiple_of(n * TILE, TILE), TILE)
            part = lax.dot_general(
                feat[rows, :],
                down[source],
                (((1,), (1,)), ((), ())),
                preferred_element_type=jnp.float32,
            )
            mine = row_adapter[rows, :] == 2 * source + lane_pair
            low_sum[rows, :] = jnp.where(mine, part, low_sum[rows, :])

    def z_recv(way, hop, q):
        dz(way, hop, q).wait_recv()

    def z_forward(way, hop, q):
        z_recv(way, hop - 1, q)
        start(dz(way, hop, q))

    for i in range(7):
        start(dy(i))
    for i in range(7):
        start(wy(i))
    start(feat_copy)

    locals_[2].wait()
    for i in range(7):
        dy(i).wait_recv()
    for n in range(3):
        start(dx(n))
    pass_w(0)
    for n in range(3):
        dx(n).wait_recv()
    for q in range(2):
        for way in range(2):
            start(dz(way, 0, q))
    pass_w(1)
    pass_w(2)
    pass_w(3)
    pass_w(4)
    pass_w(5)
    pass_w(6)
    pass_w(OWN)
    locals_[0].wait()
    feat_copy.wait_recv()
    low_part(z)
    have_w(0)
    add_up(0, 0, 0, 0)
    add_up(0, 1, 0, 1)
    for way in range(2):
        z_forward(way, 1, 0)
    have_w(1)
    add_up(1, 0, 1, 1)
    add_up(1, 0, 1, 0)
    for way in range(2):
        z_forward(way, 1, 1)
    have_w(2)
    add_up(2, 1, 1, 0)
    add_up(2, 1, 1, 1)
    low_part(mod(z - 1, NZ))
    for way in range(2):
        z_forward(way, 2, 0)
    have_w(3)
    add_up(3, 0, 2, 1)
    add_up(3, 0, 2, 0)
    have_w(4)
    for way in range(2):
        z_forward(way, 2, 1)
    add_up(4, 1, 2, 0)
    add_up(4, 1, 2, 1)
    low_part(mod(z + 1, NZ))
    z_forward(0, 3, 0)
    z_recv(1, 2, 0)
    have_w(5)
    add_up(5, 0, 3, 1)
    add_up(5, 0, 3, 0)
    have_w(6)
    add_up(6, 1, 3, 0)
    add_up(6, 1, 3, 1)
    low_part(mod(z - 2, NZ))
    low_part(mod(z + 2, NZ))
    z_forward(1, 3, 1)
    z_recv(0, 2, 1)
    have_w(OWN)
    low_part(mod(z - 3, NZ))
    low_part(mod(z + 3, NZ))
    z_recv(0, 3, 0)
    z_recv(1, 3, 1)
    low_part(mod(z + 4, NZ))

    @pl.loop(0, ROWS // TILE)
    def _(n):
        rows = pl.ds(pl.multiple_of(n * TILE, TILE), TILE)
        position = lax.div(lane, 16) * 16 + c * 8 + lax.rem(lane, 8)
        kept = position.astype(jnp.float32) < row_rank[rows, :]
        mine = jnp.where(kept, low_sum[rows, :], 0.0)
        other = jnp.where(c == 0, pltpu.roll(mine, 120, 1), pltpu.roll(mine, 8, 1))
        both = jnp.where(lane_pair == c, mine + other, 0.0)
        low_send[rows, :] = both.astype(jnp.bfloat16)

    for d in range(1, NT):
        start(lr(d))
    total = low_send[my_low, :].astype(jnp.float32)
    for d in range(1, NT):
        lr(d).wait_recv()
    for d in range(1, NT):
        total = total + low_recv[d].astype(jnp.float32)
    low[my_low, :] = total.astype(jnp.bfloat16)
    for d in range(1, NT):
        start(lg(d))

    for way in range(2):
        for half in range(2):
            rs(way, 3, half).wait_recv()

    @pl.loop(0, ROWS // TILE)
    def _(n):
        rows = pl.ds(pl.multiple_of(n * TILE, TILE), TILE)
        part = jnp.dot(feat[rows, :], weight[OWN], preferred_element_type=jnp.float32)
        recv32[0, rows, :] = part + (recv32[0, rows, :] + recv32[1, rows, :])

    locals_[3].wait()
    for d in range(1, NT):
        lg(d).wait_recv()

    @pl.loop(0, ROWS // TILE)
    def _(n):
        rows = pl.ds(pl.multiple_of(n * TILE, TILE), TILE)
        code = low[rows, :].astype(jnp.float32)
        ids = row_adapter[rows, :]
        spread = [
            jnp.where(ids == a, code, 0.0).astype(jnp.bfloat16) for a in range(ADAPTERS)
        ]
        update = jnp.dot(
            jnp.concatenate(spread, axis=1), up[...], preferred_element_type=jnp.float32
        )
        scale = 4.0 / jnp.sqrt(row_rank[rows, :])
        out_ref[rows, :] = (recv32[0, rows, :] + scale * update).astype(jnp.bfloat16)

    for copy in sent:
        copy.wait_send()


def body(features, key_value_weight, adapter_down_factors, adapter_up_factors, row_adapter_index, ranks):
    down = adapter_down_factors.transpose(1, 2, 0).reshape(ADAPTERS * 8, NY * KB)
    up = adapter_up_factors.reshape(ADAPTERS * RANK, COLS)
    index = row_adapter_index.reshape(ROWS // 128, 128)
    vmem, any_ = pl.BlockSpec(memory_space=pltpu.VMEM), pl.BlockSpec(memory_space=pl.ANY)
    bf16, f32 = jnp.bfloat16, jnp.float32
    dma = pltpu.SemaphoreType.DMA
    return pl.pallas_call(
        kernel,
        out_shape=jax.ShapeDtypeStruct((ROWS, COLS), bf16),
        in_specs=[any_, any_, any_, any_, vmem, pl.BlockSpec(memory_space=pltpu.SMEM)],
        out_specs=vmem,
        scratch_shapes=[
            pltpu.VMEM((ROWS, KB), bf16),
            pltpu.VMEM((NY, KB, COLS), bf16),
            pltpu.VMEM((NZ, NY * 16, KB), bf16),
            pltpu.VMEM((ADAPTERS * RANK, COLS), bf16),
            pltpu.VMEM((2, 3, ROWS, COLS), bf16),
            pltpu.VMEM((2, ROWS, COLS), f32),
            pltpu.VMEM((2, 3, ROWS, COLS), bf16),
            pltpu.VMEM((2, ROWS, COLS), f32),
            pltpu.VMEM((ROWS, 128), jnp.int32),
            pltpu.VMEM((ROWS, 128), f32),
            pltpu.VMEM((ROWS, 128), f32),
            pltpu.VMEM((ROWS, 128), bf16),
            pltpu.VMEM((NT, LOWROWS, 128), bf16),
            pltpu.VMEM((ROWS, 128), bf16),
            dma((4,)),
            dma((2,)),
            dma((2, 7)),
            dma((2, 8, 3)),
            dma((2, 7)),
            dma((2, 3)),
            dma((2, 2, 4, 2)),
            dma((2, 2, 4, 2)),
            dma((2, NT)),
            dma((2, NT)),
        ],
        compiler_params=pltpu.CompilerParams(
            collective_id=0, has_side_effects=True, vmem_limit_bytes=40 << 20
        ),
        cost_estimate=pl.CostEstimate(
            flops=2 * ROWS * KB * 2048 + 2 * ROWS * 2048 * COLS,
            bytes_accessed=8 << 20,
            transcendentals=0,
        ),
    )(features, key_value_weight, down, up, index, ranks)


def solution(mesh):
    in_specs = (
        P("dp", "tensor"),
        P(None, "tensor"),
        P(None, None, "tensor"),
        P(None, None, "tensor"),
        P("dp"),
        P(),
    )
    out_specs = P("dp", "tensor")
    return jax.shard_map(body, mesh=mesh, in_specs=in_specs, out_specs=out_specs, check_vma=False)
```

time: 161 us -> 87.5 us (0.54)
  waiting for transfers between devices: 104 us -> 0 us
  Pallas kernels: 0 us -> 79.7 us
  matrix products: 24 us -> 0 us
  blocking collectives: 16.3 us -> 0 us
  between operations: 13.4 us -> 0.02 us
  local copies, waits for them, and re-layouts: 0.14 us -> 7.49 us
  other arithmetic: 2.21 us -> 0 us
    all_gather x1 -> x0, waiting for transfers between devices: 104 us -> none  [body(): piece = lax.all_gather(features, 'tensor', axis=1, tiled=True)]
    pallas_call x0 -> x1, Pallas kernels: none -> 79.7 us  [body(): pl.pallas_call(kernel, out_shape=jax.ShapeDtypeStruct((ROWS, COLS), bf16)...]
    dot_general x3 -> x0, matrix products: 24 us -> none  [the longest x1 11.5 us: body(): jnp.dot(piece, flattened_down_factors, preferred_element_type=jnp.float32)]
    all_gather x1 -> x0, blocking collectives: 16.3 us -> none  [body(): low = lax.all_gather(local_low, 'tensor', axis=1, tiled=True)]
    unnamed x4 -> x13, local copies, waits for them, and re-layouts: 0.01 us -> 7.49 us
  transfers between devices with their start and end apart: 1 -> 0, of which waited for: 1 -> 0; matrix products, arithmetic and copies ran while one was open for 1% -> 0% of each run, Pallas kernels for 0% -> 0%
where the time goes in v1:
time: 87.5 us; the launch traced here: 87.2 us
  Pallas kernels  79.7 us (91%)
  local copies, waits for them, and re-layouts  7.49 us (9%)
    pallas_call x1, Pallas kernels, body(): pl.pallas_call(kernel, out_shape=jax.ShapeDtypeStruct((ROWS, COLS), bf16)...  79.7 us
    unnamed x13, local copies, waits for them, and re-layouts  7.49 us

profile of v1, /device:TPU:1, one launch (start us, length us, event | category | flops | bytes accessed | tf_op | source)
XLA Modules:
  0.0 87.2 jit_solution(18201576302983221861)
XLA Ops:
  0.0 0.0 copy-start
  0.0 1.6 %copy-done = bf16[8192,128]{1,0:T(8,128)(2,1)S(1)} copy-done((bf16[8192,128]{1,0:T(8,128)(2,1)S(1)}, bf16[8192,128]{1,0:T(8,128)(2,1)}, u32[]{:S(2)}) %copy-start) | copy-done | bytes 2097176
  1.6 0.0 copy-start.1
  1.6 1.6 %copy-done.1 = bf16[8192,16,8]{0,2,1:T(8,128)(2,1)S(1)} copy-done((bf16[8192,16,8]{0,2,1:T(8,128)(2,1)S(1)}, bf16[8192,16,8]{0,2,1:T(8,128)(2,1)}, u32[]{:S(2)}) %copy-start.1) | copy-done | bytes 2097176
  3.2 0.0 copy-start.2
  3.2 1.2 %copy-done.2 = bf16[1024,512]{1,0:T(8,128)(2,1)S(1)} copy-done((bf16[1024,512]{1,0:T(8,128)(2,1)S(1)}, bf16[1024,512]{1,0:T(8,128)(2,1)}, u32[]{:S(2)}) %copy-start.2) | copy-done | bytes 1048600
  4.4 0.0 copy-start.3
  4.4 1.0 %copy-done.3 = bf16[16,128,128]{2,1,0:T(8,128)(2,1)S(1)} copy-done((bf16[16,128,128]{2,1,0:T(8,128)(2,1)S(1)}, bf16[16,128,128]{2,1,0:T(8,128)(2,1)}, u32[]{:S(2)}) %copy-start.3) | copy-done | bytes 524312
  5.5 0.0 copy-start.4
  5.5 0.7 copy-done.4
  6.1 0.0 copy-start.5
  6.1 0.7 copy-done.5
  6.8 79.7 %shard_map.64 = bf16[1024,128]{1,0:T(8,128)(2,1)S(1)} custom-call(bf16[1024,512]{1,0:T(8,128)(2,1)S(1)} %copy-done.2, bf16[8192,128]{1,0:T(8,128)(2,1)S(1)} %copy-done, bf16[128,8192]{1,0:T(8,128)(2,1)S(1)} %bitcast.5, bf16[2048,128]{1,0:T(8,128)(2,1)S(1)} %bitcast.6, s32[8,128]{1,0:T(8,128)S(1)} %bitcast.7, s32[16]{0:T(128)S(1)} %copy-done.5), custom_call_target="tpu_custom_call" | custom-call | flops 4831838208 | bytes 8388608 | tf_op jit(solution)/shard_map/pallas_call | solution.py:365
  86.5 0.7 copy.8
Async XLA Ops:
  0.0 1.6 %copy-start = (bf16[8192,128]{1,0:T(8,128)(2,1)S(1)}, bf16[8192,128]{1,0:T(8,128)(2,1)}, u32[]{:S(2)}) copy-start(bf16[8192,128]{1,0:T(8,128)(2,1)} %weight_hbm.1) | copy-start | bytes 6291460
  1.6 1.6 %copy-start.1 = (bf16[8192,16,8]{0,2,1:T(8,128)(2,1)S(1)}, bf16[8192,16,8]{0,2,1:T(8,128)(2,1)}, u32[]{:S(2)}) copy-start(bf16[8192,16,8]{0,2,1:T(8,128)(2,1)} %param.8) | copy-start | bytes 6291460
  3.2 1.2 %copy-start.2 = (bf16[1024,512]{1,0:T(8,128)(2,1)S(1)}, bf16[1024,512]{1,0:T(8,128)(2,1)}, u32[]{:S(2)}) copy-start(bf16[1024,512]{1,0:T(8,128)(2,1)} %feat_hbm.1) | copy-start | bytes 3145732
  4.4 1.0 %copy-start.3 = (bf16[16,128,128]{2,1,0:T(8,128)(2,1)S(1)}, bf16[16,128,128]{2,1,0:T(8,128)(2,1)}, u32[]{:S(2)}) copy-start(bf16[16,128,128]{2,1,0:T(8,128)(2,1)} %param.9) | copy-start | bytes 1572868
  5.5 0.7 copy-start.4
  6.1 0.7 copy-start.5

commit v2 on v1

v2 whole, which is shorter than its diff:
```python
import functools

import jax
import jax.numpy as jnp
from jax import lax
from jax.experimental import pallas as pl
from jax.experimental.pallas import tpu as pltpu
from jax.sharding import PartitionSpec as P

MESH = pl.DeviceIdType.MESH
NX, NY, NZ, NT = 4, 8, 8, 16
ROWS = 1024
HALF = ROWS // 2
KB = 1024
KX = KB // NX
COLS = 128
ADAPTERS, RANK = 16, 128
LOWROWS = ROWS // NT
PAIR = LOWROWS // 2
TILE = 256

OFFSETS = (4, 3, -3, 2, -2, 1, -1)
UP, DOWN = (0, 1, 3, 5), (0, 2, 4, 6)
LONG = (0, 1)
X_HOPS = (1, -1, 2)


def mod(value, size):
    return lax.rem(value + size, size)


def kernel(
    feat_hbm,
    weight_hbm,
    down_hbm,
    up_hbm,
    index_hbm,
    ranks_hbm,
    out_ref,
    feat,
    weight,
    own_weight,
    down,
    up,
    index_ref,
    ranks_ref,
    send16,
    send32,
    recv16,
    recv32,
    row_adapter,
    row_rank,
    low_sum,
    low_send,
    low_recv,
    low,
    base,
    local_sem,
    feat_sem,
    wy_sem,
    wx_sem,
    dy_sem,
    dx_sem,
    dz_sem,
    sum_sem,
    lr_sem,
    lg_sem,
    lh_sem,
):
    g, t = lax.axis_index("dp"), lax.axis_index("tensor")
    z, x = lax.div(g, NX), lax.rem(g, NX)
    y, c = lax.div(t, 2), lax.rem(t, 2)

    def at(dz=0, dx=0, dy=0):
        return (mod(z + dz, NZ) * NX + mod(x + dx, NX), mod(y + dy, NY) * 2 + c)

    def line(n):
        return (g, mod(y + n // 2, NY) * 2 + (c if n % 2 == 0 else 1 - c))

    sibling = line(1)

    barrier = pltpu.get_barrier_semaphore()
    for n in range(1, NT):
        pl.semaphore_signal(barrier, inc=1, device_id=line(n), device_id_type=MESH)
    for d in X_HOPS:
        pl.semaphore_signal(barrier, inc=1, device_id=at(dx=d), device_id_type=MESH)
    for d in (1, -1):
        pl.semaphore_signal(barrier, inc=1, device_id=at(dz=d), device_id_type=MESH)

    def local(n, src, dst):
        return pltpu.make_async_copy(src, dst, local_sem.at[n])

    def remote(src, dst, sems, n, device):
        return pltpu.make_async_remote_copy(
            src_ref=src,
            dst_ref=dst,
            send_sem=sems.at[(0, *n)],
            recv_sem=sems.at[(1, *n)],
            device_id=device,
            device_id_type=MESH,
        )

    my_k = pl.ds(pl.multiple_of(x * KX, KX), KX)
    half_k = pl.ds(pl.multiple_of(c * (KB // 2), KB // 2), KB // 2)
    chip_k = pl.ds(pl.multiple_of(y * KB, KB), KB)

    def down_k(chip, k):
        return pl.ds(pl.multiple_of(chip * KB + k * 128, 128), 128)

    own_rows, other_rows = pl.ds(0, 16), pl.ds(16, NY * 16 - 16)
    locals_ = [
        local(0, feat_hbm, feat.at[:, half_k]),
        local(1, weight_hbm.at[chip_k, :], own_weight),
        local(2, up_hbm, up),
        local(3, index_hbm, index_ref),
        local(4, ranks_hbm, ranks_ref),
        *[
            local(5 + k, down_hbm.at[:, :, down_k(y, k)], down.at[k, :, own_rows])
            for k in range(KB // 128)
        ],
    ]
    for copy in locals_:
        copy.start()

    pl.semaphore_wait(barrier, NT - 1 + len(X_HOPS) + 2)

    feat_copy = remote(feat_hbm, feat.at[:, half_k], feat_sem, (), sibling)

    def wy(i):
        to = mod(y - OFFSETS[i], NY)
        src = weight_hbm.at[pl.ds(pl.multiple_of(to * KB + x * KX, KX), KX), :]
        return remote(src, weight.at[i, my_k, :], wy_sem, (i,), at(dy=-OFFSETS[i]))

    def wx(i, n):
        part = weight.at[i, my_k, :]
        return remote(part, part, wx_sem, (i, n), at(dx=X_HOPS[n]))

    def dy(i, h):
        to = mod(y - OFFSETS[i], NY)
        src = down_hbm.at[z, :, down_k(to, 2 * x + h)]
        dst = down.at[2 * x + h, z, pl.ds(OFFSETS[i] % NY * 16, 16)]
        return remote(src, dst, dy_sem, (i, h), at(dy=-OFFSETS[i]))

    def dx(n):
        part = down.at[pl.ds(2 * x, 2), z, other_rows]
        return remote(part, part, dx_sem, (n,), at(dx=X_HOPS[n]))

    def dz(way, hop, part):
        sign = 1 - 2 * way
        of = mod(x + (0, -1, 1, 2)[part], NX)
        ref = down.at[pl.ds(2 * of, 2), mod(z - sign * hop, NZ), other_rows]
        return remote(ref, ref, dz_sem, (way, hop, part), at(dz=sign))

    def rs(way, step, half):
        if step == 3 and half == LONG[way]:
            src, dst = send32.at[way], recv32.at[way]
        else:
            rows = pl.ds(half * HALF, HALF)
            src, dst = send16.at[way, step, rows], recv16.at[way, step, rows]
        return remote(src, dst, sum_sem, (way, step, half), at(dy=1 - 2 * way))

    def lr(n):
        to = mod(y + n // 2, NY), c if n % 2 == 0 else 1 - c
        return remote(low_send.at[to], low_recv.at[n], lr_sem, (n,), line(n))

    def lg(d):
        part = low.at[y, c]
        return remote(part, part, lg_sem, (d,), at(dy=d))

    def lh():
        part = low.at[:, c]
        return remote(part, part, lh_sem, (), sibling)

    sent, late = [], []

    def start(copy, among=sent):
        copy.start()
        among.append(copy)

    def drain(copies):
        for copy in copies:
            copy.wait_send()
        copies.clear()

    def pass_w(i):
        wy(i).wait_recv()
        for n in (2, 0, 1):
            start(wx(i, n))

    def have_w(i):
        for n in range(3):
            wx(i, n).wait_recv()

    def add_up(i, way, step, half):
        before = step >= 2 or (step == 1 and half == LONG[way])
        if before:
            rs(way, step - 1, half).wait_recv()

        @pl.loop(0, HALF // TILE)
        def _(n):
            rows = pl.ds(pl.multiple_of(half * HALF + n * TILE, TILE), TILE)
            part = jnp.dot(feat[rows, :], weight[i], preferred_element_type=jnp.float32)
            if before:
                part = part + recv16[way, step - 1, rows, :].astype(jnp.float32)
            if step == 3 and half == LONG[way]:
                send32[way, pl.ds(pl.multiple_of(n * TILE, TILE), TILE), :] = part
            else:
                send16[way, step, rows, :] = part.astype(jnp.bfloat16)

        start(rs(way, step, half), late if step == 3 else sent)

    lane = lax.broadcasted_iota(jnp.int32, (TILE, 128), 1)
    lane_pair = lax.rem(lax.div(lane, 8), 2)
    pair_lane = lax.rem(
        lax.div(lax.broadcasted_iota(jnp.int32, (TILE // 128, 2, PAIR, 128), 3), 8), 2
    )

    def tile_of(ref, n):
        return ref[pl.ds(n * (TILE // 128), TILE // 128)].reshape(TILE, 128)

    def low_part(back, other_back):
        first, second = mod(z - back, NZ), mod(z - other_back, NZ)
        factors = jnp.concatenate(
            [
                jnp.concatenate([down[k, source] for k in range(KB // 128)], axis=1)
                for source in (first, second)
            ],
            axis=0,
        )

        @pl.loop(0, ROWS // TILE)
        def _(n):
            rows = pl.ds(pl.multiple_of(n * TILE, TILE), TILE)
            part = lax.dot_general(
                feat[rows, :],
                factors,
                (((1,), (1,)), ((), ())),
                preferred_element_type=jnp.float32,
            )
            ids = tile_of(row_adapter, n)
            total = low_sum[rows, :]
            for source, columns in ((first, part[:, :128]), (second, part[:, 128:])):
                total = jnp.where(ids == 2 * source + lane_pair, columns, total)
            low_sum[rows, :] = total

    def z_got(way, hop, part):
        dz(way, hop, part).wait_recv()
        if hop < 2 or (hop == 2 and part in ((0, 1), (2, 3))[way]):
            start(dz(way, hop + 1, part))

    def low_codes():
        @pl.loop(0, ROWS // TILE)
        def _(n):
            rows = pl.ds(pl.multiple_of(n * TILE, TILE), TILE)
            mine = pltpu.roll(low_sum[rows, :], 16 * y, 1)
            position = lax.div(lane, 16) * 16 + c * 8 + lax.rem(lane, 8)
            kept = position.astype(jnp.float32) < tile_of(row_rank, n)
            mine = jnp.where(kept, mine, 0.0)
            across = jnp.where(lane_pair == 0, pltpu.roll(mine, 120, 1), pltpu.roll(mine, 8, 1))
            both = (mine + across).reshape(TILE // 128, 2, 2, PAIR, 128)
            pair = jnp.where(pair_lane == 0, both[:, :, 0], both[:, :, 1])
            low_send[pl.ds(n * (TILE // 128), TILE // 128)] = pair.astype(jnp.bfloat16)

        drain(sent)
        for n in range(1, NT):
            start(lr(n))

    def low_total():
        totals = [low_send[y, c].astype(jnp.float32), None]
        for n in range(1, NT):
            lr(n).wait_recv()
        for n in range(1, NT):
            part = low_recv[n].astype(jnp.float32)
            totals[n % 2] = part if totals[n % 2] is None else totals[n % 2] + part
        even = jnp.where(c == 0, totals[0], totals[1])
        odd = jnp.where(c == 0, totals[1], totals[0])
        first = jnp.where(lane_pair[:PAIR] == 0, even, pltpu.roll(odd, 8, 1))
        second = jnp.where(lane_pair[:PAIR] == 0, pltpu.roll(even, 120, 1), odd)
        low[y, c, :PAIR] = first.astype(jnp.bfloat16)
        low[y, c, PAIR:] = second.astype(jnp.bfloat16)
        drain(sent)
        for d in range(1, NY):
            start(lg(d))

    def own_part():
        locals_[1].wait()

        @pl.loop(0, ROWS // TILE)
        def _(n):
            rows = pl.ds(pl.multiple_of(n * TILE, TILE), TILE)
            part = jnp.dot(feat[rows, :], own_weight[...], preferred_element_type=jnp.float32)
            base[pl.ds(n * (TILE // 128), TILE // 128)] = part.reshape(TILE // 128, 2, LOWROWS, 128)

    def all_parts():
        for way in range(2):
            for half in range(2):
                rs(way, 3, half).wait_recv()
        for half in range(2):
            rows = slice(half * HALF, (half + 1) * HALF)
            chips = slice(half * NY // 2, (half + 1) * NY // 2)
            total = base[chips]
            for way in range(2):
                if half == LONG[way]:
                    total += recv32[way].reshape(total.shape)
                else:
                    total += recv16[way, 3, rows, :].astype(jnp.float32).reshape(total.shape)
            base[chips] = total
        drain(late)

    def finish(core):
        @pl.loop(0, NY * LOWROWS // TILE)
        def _(n):
            group = (pl.ds(n * (TILE // LOWROWS), TILE // LOWROWS), core)
            code = low[group].reshape(TILE, 128).astype(jnp.float32)
            ids = row_adapter[group].reshape(TILE, 128)
            spread = [
                jnp.where(ids == a, code, 0.0).astype(jnp.bfloat16) for a in range(ADAPTERS)
            ]
            update = jnp.dot(
                jnp.concatenate(spread, axis=1), up[...], preferred_element_type=jnp.float32
            )
            scale = 4.0 / jnp.sqrt(row_rank[group])
            total = base[group] + scale * update.reshape(scale.shape)
            out_ref[group] = total.astype(jnp.bfloat16)

    for i in range(7):
        for h in range(2):
            start(dy(i, h))
    for i in range(7):
        start(wy(i))
    start(feat_copy)
    locals_[3].wait()
    locals_[4].wait()
    for r in range(ROWS // 128):
        ids = index_ref[r : r + 1, :].astype(jnp.float32)
        spread = jnp.transpose(jnp.broadcast_to(ids, (128, 128)))
        row_adapter[r] = spread.astype(jnp.int32).reshape(2, LOWROWS, 128)

    @pl.loop(0, ROWS // 128)
    def _(r):
        ids = row_adapter[r]
        rank = jnp.zeros((2, LOWROWS, 128), jnp.float32)
        for a in range(ADAPTERS):
            rank = jnp.where(ids == a, ranks_ref[a].astype(jnp.float32), rank)
        row_rank[r] = rank

    low_sum[...] = jnp.zeros_like(low_sum)
    for i in range(7):
        for h in range(2):
            dy(i, h).wait_recv()
    for n in (2, 0, 1):
        start(dx(n))
    for way in range(2):
        start(dz(way, 0, 0))
    locals_[0].wait()
    feat_copy.wait_recv()
    own_part()
    pass_w(0)
    z_got(0, 0, 0)
    z_got(1, 0, 0)
    for n in range(3):
        dx(n).wait_recv()
    for part in (1, 2, 3):
        for way in range(2):
            start(dz(way, 0, part))
    pass_w(1)
    pass_w(2)
    z_got(0, 1, 0)
    z_got(1, 1, 0)
    pass_w(3)
    z_got(0, 0, 1)
    z_got(1, 0, 1)
    pass_w(4)
    pass_w(5)
    pass_w(6)
    z_got(0, 0, 2)
    z_got(1, 0, 2)
    have_w(0)
    add_up(0, 0, 0, 0)
    add_up(0, 1, 0, 1)
    z_got(0, 0, 3)
    z_got(1, 0, 3)
    have_w(1)
    add_up(1, 0, 1, 1)
    z_got(0, 2, 0)
    z_got(1, 2, 0)
    for k in range(KB // 128):
        locals_[5 + k].wait()
    low_part(0, 1)
    z_got(0, 1, 1)
    z_got(1, 1, 1)
    have_w(2)
    add_up(2, 1, 1, 0)
    z_got(0, 1, 2)
    z_got(1, 1, 2)
    add_up(1, 0, 1, 0)
    add_up(2, 1, 1, 1)
    z_got(0, 1, 3)
    z_got(1, 1, 3)
    have_w(3)
    low_part(7, 2)
    z_got(0, 3, 0)
    z_got(1, 2, 1)
    add_up(3, 0, 2, 1)
    z_got(0, 2, 1)
    z_got(1, 2, 2)
    have_w(4)
    add_up(4, 1, 2, 0)
    z_got(0, 2, 2)
    z_got(1, 2, 3)
    add_up(3, 0, 2, 0)
    have_w(5)
    z_got(0, 2, 3)
    low_part(6, 3)
    z_got(0, 3, 1)
    z_got(1, 3, 2)
    add_up(4, 1, 2, 1)
    z_got(1, 3, 3)
    have_w(6)
    add_up(5, 0, 3, 1)
    add_up(6, 1, 3, 0)
    low_part(5, 4)
    low_codes()
    add_up(5, 0, 3, 0)
    add_up(6, 1, 3, 1)
    low_total()
    all_parts()
    for d in range(1, NY):
        lg(d).wait_recv()
    start(lh())
    locals_[2].wait()
    finish(c)
    lh().wait_recv()
    finish(1 - c)
    drain(sent)


def body(features, key_value_weight, adapter_down_factors, adapter_up_factors, row_adapter_index, ranks):
    down = adapter_down_factors.transpose(1, 2, 0).reshape(NZ, 16, NY * KB)
    up = adapter_up_factors.reshape(ADAPTERS * RANK, COLS)
    index = row_adapter_index.reshape(ROWS // 128, 128)
    vmem, any_ = pl.BlockSpec(memory_space=pltpu.VMEM), pl.BlockSpec(memory_space=pl.ANY)
    bf16, f32 = jnp.bfloat16, jnp.float32
    dma = pltpu.SemaphoreType.DMA
    return pl.pallas_call(
        kernel,
        out_shape=jax.ShapeDtypeStruct((NY, 2, LOWROWS, COLS), bf16),
        in_specs=[any_] * 6,
        out_specs=vmem,
        scratch_shapes=[
            pltpu.VMEM((ROWS, KB), bf16),
            pltpu.VMEM((NY - 1, KB, COLS), bf16),
            pltpu.VMEM((KB, COLS), bf16),
            pltpu.VMEM((KB // 128, NZ, NY * 16, 128), bf16),
            pltpu.VMEM((ADAPTERS * RANK, COLS), bf16),
            pltpu.VMEM((ROWS // 128, 128), jnp.int32),
            pltpu.SMEM((ADAPTERS,), jnp.int32),
            pltpu.VMEM((2, 4, ROWS, COLS), bf16),
            pltpu.VMEM((2, HALF, COLS), f32),
            pltpu.VMEM((2, 4, ROWS, COLS), bf16),
            pltpu.VMEM((2, HALF, COLS), f32),
            pltpu.VMEM((NY, 2, LOWROWS, 128), jnp.int32),
            pltpu.VMEM((NY, 2, LOWROWS, 128), f32),
            pltpu.VMEM((ROWS, 128), f32),
            pltpu.VMEM((NY, 2, PAIR, 128), bf16),
            pltpu.VMEM((NT, PAIR, 128), bf16),
            pltpu.VMEM((NY, 2, LOWROWS, 128), bf16),
            pltpu.VMEM((NY, 2, LOWROWS, COLS), f32),
            dma((5 + KB // 128,)),
            dma((2,)),
            dma((2, 7)),
            dma((2, 7, 3)),
            dma((2, 7, 2)),
            dma((2, 3)),
            dma((2, 2, 4, 4)),
            dma((2, 2, 4, 2)),
            dma((2, NT)),
            dma((2, NY)),
            dma((2,)),
        ],
        compiler_params=pltpu.CompilerParams(
            collective_id=0, has_side_effects=True, vmem_limit_bytes=60 << 20
        ),
        cost_estimate=pl.CostEstimate(
            flops=2 * ROWS * KB * 2048 + 2 * ROWS * 2048 * COLS,
            bytes_accessed=8 << 20,
            transcendentals=0,
        ),
    )(features, key_value_weight, down, up, index, ranks).reshape(ROWS, COLS)


def solution(mesh):
    in_specs = (
        P("dp", "tensor"),
        P(None, "tensor"),
        P(None, None, "tensor"),
        P(None, None, "tensor"),
        P("dp"),
        P(),
    )
    out_specs = P("dp", "tensor")
    return jax.shard_map(body, mesh=mesh, in_specs=in_specs, out_specs=out_specs, check_vma=False)
```

time: 87.5 us -> 71 us (0.81)
  Pallas kernels: 79.7 us -> 69.1 us
  local copies, waits for them, and re-layouts: 7.49 us -> 1.67 us
    pallas_call x1, Pallas kernels: 79.7 us -> 69.1 us  [body(): pl.pallas_call(kernel, out_shape=jax.ShapeDtypeStruct((NY, 2, LOWROWS, CO...]
    unnamed x13 -> x1, local copies, waits for them, and re-layouts: 7.49 us -> 1.67 us
where the time goes in v2:
time: 71 us; the launch traced here: 70.8 us
  Pallas kernels  69.1 us (97%)
  local copies, waits for them, and re-layouts  1.67 us (2%)
    pallas_call x1, Pallas kernels, body(): pl.pallas_call(kernel, out_shape=jax.ShapeDtypeStruct((NY, 2, LOWROWS, CO...  69.1 us
    unnamed x1, local copies, waits for them, and re-layouts  1.67 us

profile of v2, /device:TPU:1, one launch (start us, length us, event | category | flops | bytes accessed | tf_op | source)
XLA Modules:
  0.0 70.8 jit_solution(2329638787134271299)
XLA Ops:
  0.0 69.1 %shard_map.64 = bf16[8,2,64,128]{3,2,1,0:T(8,128)(2,1)} custom-call(bf16[1024,512]{1,0:T(8,128)(2,1)} %feat_hbm.1, bf16[8192,128]{1,0:T(8,128)(2,1)} %weight_hbm.1, bf16[8,16,8192]{2,1,0:T(8,128)(2,1)} %bitcast.7, bf16[2048,128]{1,0:T(8,128)(2,1)} %bitcast.8, s32[8,128]{1,0:T(8,128)} %bitcast.9, s32[16]{0:T(128)} %ranks_hbm.1), custom_call_target="tpu_custom_call" | custom-call | flops 4831838208 | bytes 8388608 | tf_op jit(solution)/shard_map/pallas_call | solution.py:445
  69.1 1.7 %copy.8 = bf16[1024,128]{1,0:T(8,128)(2,1)} copy(bf16[1024,128]{1,0:T(8,128)(2,1)} %bitcast.6) | data formatting | bytes 524288

commit v3 on v2

--- a/solution.py
+++ b/solution.py
@@ -119,7 +119,7 @@
             for k in range(KB // 128)
         ],
     ]
-    for copy in locals_:
+    for copy in locals_[3:5]:
         copy.start()
 
     pl.semaphore_wait(barrier, NT - 1 + len(X_HOPS) + 2)
@@ -171,7 +171,7 @@
         part = low.at[:, c]
         return remote(part, part, lh_sem, (), sibling)
 
-    sent, late = [], []
+    sent, late, codes = [], [], []
 
     def start(copy, among=sent):
         copy.start()
@@ -212,7 +212,7 @@
     lane = lax.broadcasted_iota(jnp.int32, (TILE, 128), 1)
     lane_pair = lax.rem(lax.div(lane, 8), 2)
     pair_lane = lax.rem(
-        lax.div(lax.broadcasted_iota(jnp.int32, (TILE // 128, 2, PAIR, 128), 3), 8), 2
+        lax.div(lax.broadcasted_iota(jnp.int32, (2, PAIR, 128), 2), 8), 2
     )
 
     def tile_of(ref, n):
@@ -249,21 +249,22 @@
             start(dz(way, hop + 1, part))
 
     def low_codes():
-        @pl.loop(0, ROWS // TILE)
-        def _(n):
-            rows = pl.ds(pl.multiple_of(n * TILE, TILE), TILE)
+        position = lax.div(lane, 16) * 16 + c * 8 + lax.rem(lane, 8)
+        for d in (4, 3, 5, 2, 6, 1, 7, 0):
+            chip = mod(y + d, NY)
+            rows = pl.ds(pl.multiple_of(chip * 128, 128), 128)
             mine = pltpu.roll(low_sum[rows, :], 16 * y, 1)
-            position = lax.div(lane, 16) * 16 + c * 8 + lax.rem(lane, 8)
-            kept = position.astype(jnp.float32) < tile_of(row_rank, n)
+            kept = position[:128].astype(jnp.float32) < row_rank[chip].reshape(128, 128)
             mine = jnp.where(kept, mine, 0.0)
-            across = jnp.where(lane_pair == 0, pltpu.roll(mine, 120, 1), pltpu.roll(mine, 8, 1))
-            both = (mine + across).reshape(TILE // 128, 2, 2, PAIR, 128)
-            pair = jnp.where(pair_lane == 0, both[:, :, 0], both[:, :, 1])
-            low_send[pl.ds(n * (TILE // 128), TILE // 128)] = pair.astype(jnp.bfloat16)
-
+            left, right = pltpu.roll(mine, 120, 1), pltpu.roll(mine, 8, 1)
+            both = mine + jnp.where(lane_pair[:128] == 0, left, right)
+            both = both.reshape(2, 2, PAIR, 128)
+            pair = jnp.where(pair_lane == 0, both[:, 0], both[:, 1])
+            low_send[chip] = pair.astype(jnp.bfloat16)
+            for n in (2 * d, 2 * d + 1):
+                if n:
+                    start(lr(n), codes)
         drain(sent)
-        for n in range(1, NT):
-            start(lr(n))
 
     def low_total():
         totals = [low_send[y, c].astype(jnp.float32), None]
@@ -278,9 +279,9 @@
         second = jnp.where(lane_pair[:PAIR] == 0, pltpu.roll(even, 120, 1), odd)
         low[y, c, :PAIR] = first.astype(jnp.bfloat16)
         low[y, c, PAIR:] = second.astype(jnp.bfloat16)
-        drain(sent)
         for d in range(1, NY):
             start(lg(d))
+        drain(codes)
 
     def own_part():
         locals_[1].wait()
@@ -329,6 +330,8 @@
     for i in range(7):
         start(wy(i))
     start(feat_copy)
+    for copy in locals_[:3] + locals_[5:]:
+        copy.start()
     locals_[3].wait()
     locals_[4].wait()
     for r in range(ROWS // 128):
@@ -370,55 +373,55 @@
     pass_w(3)
     z_got(0, 0, 1)
     z_got(1, 0, 1)
+    have_w(0)
+    add_up(0, 0, 0, 0)
     pass_w(4)
     pass_w(5)
+    add_up(0, 1, 0, 1)
     pass_w(6)
     z_got(0, 0, 2)
     z_got(1, 0, 2)
-    have_w(0)
-    add_up(0, 0, 0, 0)
-    add_up(0, 1, 0, 1)
+    have_w(1)
+    add_up(1, 0, 1, 1)
     z_got(0, 0, 3)
     z_got(1, 0, 3)
-    have_w(1)
-    add_up(1, 0, 1, 1)
     z_got(0, 2, 0)
     z_got(1, 2, 0)
     for k in range(KB // 128):
         locals_[5 + k].wait()
     low_part(0, 1)
+    have_w(2)
+    add_up(2, 1, 1, 0)
+    add_up(1, 0, 1, 0)
     z_got(0, 1, 1)
     z_got(1, 1, 1)
-    have_w(2)
-    add_up(2, 1, 1, 0)
+    add_up(2, 1, 1, 1)
     z_got(0, 1, 2)
     z_got(1, 1, 2)
-    add_up(1, 0, 1, 0)
-    add_up(2, 1, 1, 1)
+    have_w(3)
     z_got(0, 1, 3)
     z_got(1, 1, 3)
-    have_w(3)
     low_part(7, 2)
+    add_up(3, 0, 2, 1)
+    have_w(4)
+    add_up(4, 1, 2, 0)
     z_got(0, 3, 0)
     z_got(1, 2, 1)
-    add_up(3, 0, 2, 1)
     z_got(0, 2, 1)
     z_got(1, 2, 2)
-    have_w(4)
-    add_up(4, 1, 2, 0)
+    add_up(3, 0, 2, 0)
+    have_w(5)
     z_got(0, 2, 2)
     z_got(1, 2, 3)
-    add_up(3, 0, 2, 0)
-    have_w(5)
     z_got(0, 2, 3)
     low_part(6, 3)
+    add_up(4, 1, 2, 1)
+    have_w(6)
+    add_up(5, 0, 3, 1)
     z_got(0, 3, 1)
     z_got(1, 3, 2)
-    add_up(4, 1, 2, 1)
+    add_up(6, 1, 3, 0)
     z_got(1, 3, 3)
-    have_w(6)
-    add_up(5, 0, 3, 1)
-    add_up(6, 1, 3, 0)
     low_part(5, 4)
     low_codes()
     add_up(5, 0, 3, 0)

time: 71 us -> 71.1 us (level)
  no operation moved by 1% of the time
where the time goes in v3:
time: 71.1 us; the launch traced here: 70.9 us
  Pallas kernels  69.3 us (97%)
  local copies, waits for them, and re-layouts  1.67 us (2%)
    pallas_call x1, Pallas kernels, body(): pl.pallas_call(kernel, out_shape=jax.ShapeDtypeStruct((NY, 2, LOWROWS, CO...  69.3 us
    unnamed x1, local copies, waits for them, and re-layouts  1.67 us

profile of v3, /device:TPU:1, one launch (start us, length us, event | category | flops | bytes accessed | tf_op | source)
XLA Modules:
  0.0 70.9 jit_solution(5983039623925959682)
XLA Ops:
  0.0 69.3 %shard_map.64 = bf16[8,2,64,128]{3,2,1,0:T(8,128)(2,1)} custom-call(bf16[1024,512]{1,0:T(8,128)(2,1)} %feat_hbm.1, bf16[8192,128]{1,0:T(8,128)(2,1)} %weight_hbm.1, bf16[8,16,8192]{2,1,0:T(8,128)(2,1)} %bitcast.7, bf16[2048,128]{1,0:T(8,128)(2,1)} %bitcast.8, s32[8,128]{1,0:T(8,128)} %bitcast.9, s32[16]{0:T(128)} %ranks_hbm.1), custom_call_target="tpu_custom_call" | custom-call | flops 4831838208 | bytes 8388608 | tf_op jit(solution)/shard_map/pallas_call | solution.py:448
  69.3 1.7 %copy.8 = bf16[1024,128]{1,0:T(8,128)(2,1)} copy(bf16[1024,128]{1,0:T(8,128)(2,1)} %bitcast.6) | data formatting | bytes 524288

commit v4 on v3

--- a/solution.py
+++ b/solution.py
@@ -17,7 +17,7 @@
 ADAPTERS, RANK = 16, 128
 LOWROWS = ROWS // NT
 PAIR = LOWROWS // 2
-TILE = 256
+TILE = 512
 
 OFFSETS = (4, 3, -3, 2, -2, 1, -1)
 UP, DOWN = (0, 1, 3, 5), (0, 2, 4, 6)

time: 71.1 us -> 71.2 us (level)
  no operation moved by 1% of the time
where the time goes in v4:
time: 71.2 us; the launch traced here: 71.1 us
  Pallas kernels  69.4 us (97%)
  local copies, waits for them, and re-layouts  1.67 us (2%)
    pallas_call x1, Pallas kernels, body(): pl.pallas_call(kernel, out_shape=jax.ShapeDtypeStruct((NY, 2, LOWROWS, CO...  69.4 us
    unnamed x1, local copies, waits for them, and re-layouts  1.67 us

profile of v4, /device:TPU:1, one launch (start us, length us, event | category | flops | bytes accessed | tf_op | source)
XLA Modules:
  0.0 71.1 jit_solution(11297778852756782889)
XLA Ops:
  0.0 69.4 %shard_map.64 = bf16[8,2,64,128]{3,2,1,0:T(8,128)(2,1)} custom-call(bf16[1024,512]{1,0:T(8,128)(2,1)} %feat_hbm.1, bf16[8192,128]{1,0:T(8,128)(2,1)} %weight_hbm.1, bf16[8,16,8192]{2,1,0:T(8,128)(2,1)} %bitcast.7, bf16[2048,128]{1,0:T(8,128)(2,1)} %bitcast.8, s32[8,128]{1,0:T(8,128)} %bitcast.9, s32[16]{0:T(128)} %ranks_hbm.1), custom_call_target="tpu_custom_call" | custom-call | flops 4831838208 | bytes 8388608 | tf_op jit(solution)/shard_map/pallas_call | solution.py:448
  69.4 1.7 %copy.8 = bf16[1024,128]{1,0:T(8,128)(2,1)} copy(bf16[1024,128]{1,0:T(8,128)(2,1)} %bitcast.6) | data formatting | bytes 524288
